TPU v7x, 32 devices: a whole 2x2x4 slice. The times are simulated.
32 devices in a mesh: ax: 16 (over z, y, x), rad: 2 (over core).
Axes of the slice: x: 2, y: 2, z: 4, core: 2. Of those that a mesh axis runs over, the one named last changes fastest.
Arguments:
- fields: float32 [128, 5, 8, 1024], P('ax', None, None, 'rad'), may hold values from -6 to 6
Outputs:
- axial_deriv: float32 [128, 5, 8, 1024], P('ax', None, None, 'rad')
- filtered: float32 [128, 5, 8, 1024], P('ax', None, None, 'rad')
- radial_deriv: float32 [128, 5, 8, 1024], P('ax', None, None, 'rad')
All inputs are finite; a program needn't handle non-finite values.
Results may differ from a plain program's by a relative error of at most 0.0003.
Values sent between devices are 32-bit elements; how exact they have to be, the bound alone decides.
A program may use at most 128 MiB of HBM per device.

v0:
```python
import jax
import jax.numpy as jnp
from jax import lax
from jax.sharding import PartitionSpec as P

deriv_alpha = 1.0 / 3.0
filter_alpha = 0.4999
block_rows = 64


def with_halo(array, sides, width):
    for axis, dim in sides:
        size, length = (lax.axis_size(axis), array.shape[dim])
        up = [(i, (i + 1) % size) for i in range(size - 1)]
        down = [(j, i) for i, j in up]
        last = lax.slice_in_dim(array, length - width, length, axis=dim)
        initial = lax.slice_in_dim(array, 0, width, axis=dim)
        before = lax.ppermute(last, axis, up)
        after = lax.ppermute(initial, axis, down)
        array = jnp.concatenate([before, array, after], axis=dim)
    return array


def filter_weights():
    return [
        (93.0 + 70.0 * filter_alpha) / 128.0,
        (7.0 + 18.0 * filter_alpha) / 16.0,
        (-7.0 + 14.0 * filter_alpha) / 32.0,
        (1.0 - 2.0 * filter_alpha) / 16.0,
        (-1.0 + 2.0 * filter_alpha) / 128.0,
    ]


def sources(padded, count):

    def shifted(k):
        return padded[4 + k : 4 + k + count]

    deriv_rhs = 7.0 / 9.0 * (shifted(1) - shifted(-1)) + 1.0 / 36.0 * (shifted(2) - shifted(-2))
    weights = filter_weights()
    filter_rhs = weights[0] * shifted(0)
    for n in range(1, 5):
        filter_rhs = filter_rhs + weights[n] / 2.0 * (shifted(n) + shifted(-n))
    return jnp.stack([deriv_rhs, filter_rhs])


def pivots(alpha, rows):
    root = (1.0 - 4.0 * alpha * alpha) ** 0.5
    big_root = (1.0 + root) / 2.0
    ratio = (1.0 - root) / (1.0 + root)
    return big_root * (1.0 - jnp.power(ratio, rows + 2.0)) / (1.0 - jnp.power(ratio, rows + 1.0))


def tables(alpha, rows):
    length = rows.shape[-1]
    piv = pivots(alpha, rows)
    before = pivots(alpha, jnp.maximum(rows - 1.0, 0.0))
    log_fwd = jnp.log(alpha / before)
    cum_fwd = jnp.cumsum(log_fwd, axis=-1)
    log_bwd = jnp.log(alpha / piv)
    cum_bwd = jnp.cumsum(log_bwd, axis=-1)
    excl_bwd = cum_bwd - log_bwd
    index = jnp.arange(length)
    parity = ((index[:, None] - index[None, :]) % 2).astype(jnp.float32)
    signs = 1.0 - 2.0 * parity
    lower = index[:, None] >= index[None, :]
    upper = index[:, None] <= index[None, :]
    diff_fwd = jnp.minimum(cum_fwd[..., :, None] - cum_fwd[..., None, :], 0.0)
    forward = jnp.where(lower, signs * jnp.exp(diff_fwd), 0.0)
    diff_bwd = jnp.minimum(excl_bwd[..., None, :] - excl_bwd[..., :, None], 0.0)
    backward = jnp.where(upper, signs * jnp.exp(diff_bwd) / piv[..., None, :], 0.0)
    sign_in = 1.0 - 2.0 * ((index + 1) % 2).astype(jnp.float32)
    gain_in = sign_in * jnp.exp(cum_fwd)
    sign_out = 1.0 - 2.0 * ((length - index) % 2).astype(jnp.float32)
    gain_out = sign_out * jnp.exp(cum_bwd[..., length - 1 :] - excl_bwd)
    return (forward, gain_in, backward, gain_out)


def combine(earlier, later):
    return (earlier[0] * later[0], later[1] + later[0] * earlier[1])


def solve(rhs, rows, chain_forward, chain_backward):
    parts = [tables(deriv_alpha, rows), tables(filter_alpha, rows)]
    forward = jnp.stack([parts[0][0], parts[1][0]])
    gain_in = jnp.stack([parts[0][1], parts[1][1]])
    backward = jnp.stack([parts[0][2], parts[1][2]])
    gain_out = jnp.stack([parts[0][3], parts[1][3]])
    local_fwd = jnp.einsum("sbkj,sbjl->sbkl", forward, rhs, precision=lax.Precision.HIGHEST)
    incoming = chain_forward(gain_in[:, :, -1:], local_fwd[:, :, -1, :])
    eliminated = local_fwd + gain_in[..., None] * incoming[:, :, None, :]
    local_bwd = jnp.einsum("sbkj,sbjl->sbkl", backward, eliminated, precision=lax.Precision.HIGHEST)
    outgoing = chain_backward(gain_out[:, :, :1], local_bwd[:, :, 0, :])
    return local_bwd + gain_out[..., None] * outgoing[:, :, None, :]


def block_chain(coeff, offset):
    inclusive = lax.associative_scan(combine, (coeff, offset), axis=1)
    return jnp.concatenate([jnp.zeros_like(offset[:, :1]), inclusive[1][:, :-1]], axis=1)


def block_forward(coeff, offset):
    return block_chain(coeff, offset)


def block_backward(coeff, offset):
    flipped = block_chain(jnp.flip(coeff, axis=1), jnp.flip(offset, axis=1))
    return jnp.flip(flipped, axis=1)


def body(fields):
    rows_dev, count, planes, radial = fields.shape
    width = count * planes * radial
    rimmed = with_halo(fields, (("rad", 3),), 3)

    def radial_cell(k):
        return rimmed[:, :, :, 3 + k : 3 + k + radial]

    radial_deriv = (
        45.0 * (radial_cell(1) - radial_cell(-1))
        - 9.0 * (radial_cell(2) - radial_cell(-2))
        + (radial_cell(3) - radial_cell(-3))
    ) / 60.0
    flat = fields.reshape(rows_dev, width)
    lines = lax.all_to_all(flat, "ax", split_axis=1, concat_axis=0, tiled=True)
    total = lines.shape[0]
    padded = jnp.pad(lines, ((4, 4), (0, 0)))
    rhs = sources(padded, total)
    blocks = total // block_rows
    rows = jnp.arange(total, dtype=jnp.float32).reshape(blocks, block_rows)
    solved = solve(rhs.reshape(2, blocks, block_rows, -1), rows, block_forward, block_backward)
    solved = solved.reshape(2, total, -1)
    result = lax.all_to_all(solved, "ax", split_axis=1, concat_axis=2, tiled=True)
    axial_deriv = result[0].reshape(fields.shape)
    filtered = result[1].reshape(fields.shape)
    return (axial_deriv, filtered, radial_deriv)


def solution(mesh):
    in_specs = (P("ax", None, None, "rad"),)
    out_specs = (P("ax", None, None, "rad"), P("ax", None, None, "rad"), P("ax", None, None, "rad"))
    return jax.shard_map(body, mesh=mesh, in_specs=in_specs, out_specs=out_specs, check_vma=False)
```

profile of v0, /device:TPU:0, one launch (start us, length us, event | category | flops | bytes accessed | tf_op | source)
XLA Modules:
  0.0 71.7 jit_solution(13071631974729192661)
XLA Ops:
  0.6 1.3 %all_to_all.25 = f32[8,16,1280]{2,1,0:T(8,128)S(1)} reshape(f32[8,5,8,512]{3,2,1,0:T(8,128)} %param.1) | data formatting | bytes 1310720 | tf_op jit(solution)/shard_map/all_to_all | solution.py:125
  1.9 1.2 %copy.11 = f32[8,16,1280]{2,0,1:T(8,128)} copy(f32[8,16,1280]{2,1,0:T(8,128)S(1)} %all_to_all.25) | data formatting | bytes 1310720 | tf_op jit(solution)/shard_map/all_to_all | solution.py:125
  3.2 8.3 %all-to-all-start = ((f32[8,16,1280]{2,0,1:T(8,128)}), f32[8,16,1280]{2,0,1:T(8,128)S(1)}, u32[]{:S(2)}, u32[]{:S(2)}) async-start(f32[8,16,1280]{2,0,1:T(8,128)} %copy.11), calls=%async_computation | async-start | bytes 1310720 | tf_op jit(solution)/shard_map/all_to_all | solution.py:125
  11.6 0.2 reduce_window_sum.36
  11.9 0.2 reduce_window_sum.29
  12.1 0.2 reduce_window_sum.28
  12.4 0.2 reduce_window_sum.27
  12.6 0.2 slice_reduce_fusion
  12.8 0.1 fusion.39
  12.9 0.1 fusion.49
  13.0 0.2 fusion.48
  13.3 0.1 divide_select_fusion.1
  13.5 15.4 %all-to-all-done = f32[8,16,1280]{2,0,1:T(8,128)S(1)} async-done(((f32[8,16,1280]{2,0,1:T(8,128)}), f32[8,16,1280]{2,0,1:T(8,128)S(1)}, u32[]{:S(2)}, u32[]{:S(2)}) %all-to-all-start) | async-done | bytes 655392 | tf_op jit(solution)/shard_map/all_to_all | solution.py:125
  28.9 0.7 multiply_add_fusion.2
  29.6 1.2 %fusion = f32[2,2,64,1280]{3,2,1,0:T(8,128)S(1)} fusion(f32[1,2,64,1280]{3,2,1,0:T(8,128)S(1)} %bitcast.45, f32[1,2,64,1280]{3,2,1,0:T(8,128)S(1)} %bitcast.44, f32[1,2,64,64]{3,2,1,0:T(8,128)S(1)} %get-tuple-element.13, f32[1,2,64,64]{3,2,1,0:T(8,128)S(1)} %get-tuple-element.14), kind=kOutput, calls=%fused_computation | convolution fusion | flops 252002304 | bytes 2686976 | tf_op jit(solution)/shard_map/sbkj,sbjl->sbkl/dot_general | solution.py:89
  30.9 0.1 fusion.67
  31.0 1.3 %fusion.4 = f32[2,2,64,1280]{3,2,1,0:T(8,128)S(1)} fusion(f32[2,2,64,1280]{3,2,1,0:T(8,128)S(1)} %fusion, f32[2,2,1280]{2,1,0:T(2,128)S(1)} %concatenate.18, f32[2,2,64]{2,1,0:T(2,128)S(1)} %pad_maximum_fusion.1, f32[1,2,64,64]{3,2,1,0:T(8,128)S(1)} %get-tuple-element.10, f32[1,2,64,64]{3,2,1,0:T(8,128)S(1)} %get-tuple-element.9), kind=kOutput, calls=%fused_computation.5 | convolution fusion | flops 252329984 | bytes 2708480 | tf_op jit(solution)/shard_map/sbkj,sbjl->sbkl/dot_general | solution.py:92
  32.3 0.1 fusion.66
  32.5 0.3 rev.7
  32.8 0.2 multiply_add_fusion
  33.0 2.1 %copy.12 = f32[2,128,1280]{2,0,1:T(2,128)} copy(f32[2,128,1280]{2,1,0:T(8,128)S(1)} %bitcast.42) | data formatting | bytes 2621440 | tf_op jit(solution)/shard_map/reshape | solution.py:132
  35.0 0.0 copy-start
  35.0 4.5 %all-to-all-start.1 = ((f32[2,128,1280]{2,0,1:T(2,128)}), f32[2,128,1280]{2,0,1:T(2,128)S(1)}, u32[]{:S(2)}, u32[]{:S(2)}) async-start(f32[2,128,1280]{2,0,1:T(2,128)} %copy.12), calls=%async_computation.1 | async-start | bytes 2621440 | tf_op jit(solution)/shard_map/all_to_all | solution.py:133
  39.6 0.0 copy-done
  39.6 0.1 fusion.65
  39.7 1.3 %collective-permute-start = (f32[8,5,8,3]{3,2,1,0:T(8,128)S(1)}, f32[8,5,8,3]{3,2,1,0:T(8,128)S(1)}, u32[]{:S(2)}, u32[]{:S(2)}) collective-permute-start(f32[8,5,8,3]{3,2,1,0:T(8,128)S(1)} %get-tuple-element.5), channel_id=1, source_target_pairs={{1,0},{3,2},{5,4},{7,6},{9,8},{11,10},{13,12},{15,14},{17,16},{19,... | collective-permute-start | bytes 11528 | tf_op jit(solution)/shard_map/ppermute | solution.py:19
  41.0 3.0 %collective-permute-start.1 = (f32[8,5,8,3]{3,2,1,0:T(8,128)S(1)}, f32[8,5,8,3]{3,2,1,0:T(8,128)S(1)}, u32[]{:S(2)}, u32[]{:S(2)}) collective-permute-start(f32[8,5,8,3]{3,2,1,0:T(8,128)S(1)} %get-tuple-element.6), channel_id=1, source_target_pairs={{0,1},{2,3},{4,5},{6,7},{8,9},{10,11},{12,13},{14,15},{16,17},{18,... | collective-permute-start | bytes 11528 | tf_op jit(solution)/shard_map/ppermute | solution.py:18
  44.1 0.0 collective-permute-done
  44.1 0.9 %collective-permute-done.1 = f32[8,5,8,3]{3,2,1,0:T(8,128)S(1)} collective-permute-done((f32[8,5,8,3]{3,2,1,0:T(8,128)S(1)}, f32[8,5,8,3]{3,2,1,0:T(8,128)S(1)}, u32[]{:S(2)}, u32[]{:S(2)}) %collective-permute-start.1) | collective-permute-done | bytes 3872 | tf_op jit(solution)/shard_map/ppermute | solution.py:18
  45.1 2.0 %fusion.12 = f32[8,5,8,512]{3,2,1,0:T(8,128)} fusion(f32[8,5,8,512]{3,2,1,0:T(8,128)S(1)} %copy-done, f32[8,5,8,3]{3,2,1,0:T(8,128)S(1)} %collective-permute-done.1, f32[8,5,8,515]{3,2,1,0:T(8,128)S(1)} %constant_dynamic-update-slice_fusion), kind=kLoop, calls=%fused_computation.17 | loop fusion | flops 1802240 | bytes 3280640 | tf_op jit(solution)/shard_map/div | solution.py:119
  47.1 21.1 %all-to-all-done.1 = f32[2,128,1280]{2,0,1:T(2,128)S(1)} async-done(((f32[2,128,1280]{2,0,1:T(2,128)}), f32[2,128,1280]{2,0,1:T(2,128)S(1)}, u32[]{:S(2)}, u32[]{:S(2)}) %all-to-all-start.1) | async-done | bytes 1310752 | tf_op jit(solution)/shard_map/all_to_all | solution.py:133
  68.2 1.0 %fusion.64 = (f32[1,8,16,1280]{3,0,1,2:T(1,128)S(1)}, f32[1,8,16,1280]{3,0,1,2:T(1,128)S(1)}) fusion(f32[2,8,16,1280]{3,0,1,2:T(2,128)S(1)} %bitcast.41), kind=kLoop, calls=%fused_computation.122 | loop fusion | bytes 2621440 | tf_op jit(solution)/shard_map/slice | solution.py:135
  69.2 0.2 copy.14
  69.4 1.0 %reshape_squeeze.7 = f32[8,5,8,512]{3,2,1,0:T(8,128)} reshape(f32[1,8,16,1280]{3,2,1,0:T(8,128)S(1)} %copy.14) | data formatting | bytes 1310720 | tf_op jit(solution)/shard_map/reshape;squeeze | solution.py:135
  70.4 0.2 copy.13
  70.6 1.0 %reshape_squeeze.6 = f32[8,5,8,512]{3,2,1,0:T(8,128)} reshape(f32[1,8,16,1280]{3,2,1,0:T(8,128)S(1)} %copy.13) | data formatting | bytes 1310720 | tf_op jit(solution)/shard_map/reshape;squeeze | solution.py:134
  (23 shorter events, 0.4 us)
Async XLA Ops:
  3.2 25.7 %all-to-all-start = ((f32[8,16,1280]{2,0,1:T(8,128)}), f32[8,16,1280]{2,0,1:T(8,128)S(1)}, u32[]{:S(2)}, u32[]{:S(2)}) async-start(f32[8,16,1280]{2,0,1:T(8,128)} %copy.11), calls=%async_computation | async-start | bytes 1310720 | tf_op jit(solution)/shard_map/all_to_all | solution.py:125
  35.0 4.6 %copy-start = (f32[8,5,8,512]{3,2,1,0:T(8,128)S(1)}, f32[8,5,8,512]{3,2,1,0:T(8,128)}, u32[]{:S(2)}) copy-start(f32[8,5,8,512]{3,2,1,0:T(8,128)} %param.1) | copy-start | bytes 1966084
  35.0 33.1 %all-to-all-start.1 = ((f32[2,128,1280]{2,0,1:T(2,128)}), f32[2,128,1280]{2,0,1:T(2,128)S(1)}, u32[]{:S(2)}, u32[]{:S(2)}) async-start(f32[2,128,1280]{2,0,1:T(2,128)} %copy.12), calls=%async_computation.1 | async-start | bytes 2621440 | tf_op jit(solution)/shard_map/all_to_all | solution.py:133
  39.7 4.4 %collective-permute-start = (f32[8,5,8,3]{3,2,1,0:T(8,128)S(1)}, f32[8,5,8,3]{3,2,1,0:T(8,128)S(1)}, u32[]{:S(2)}, u32[]{:S(2)}) collective-permute-start(f32[8,5,8,3]{3,2,1,0:T(8,128)S(1)} %get-tuple-element.5), channel_id=1, source_target_pairs={{1,0},{3,2},{5,4},{7,6},{9,8},{11,10},{13,12},{15,14},{17,16},{19,... | collective-permute-start | bytes 11528 | tf_op jit(solution)/shard_map/ppermute | solution.py:19
  41.0 4.1 %collective-permute-start.1 = (f32[8,5,8,3]{3,2,1,0:T(8,128)S(1)}, f32[8,5,8,3]{3,2,1,0:T(8,128)S(1)}, u32[]{:S(2)}, u32[]{:S(2)}) collective-permute-start(f32[8,5,8,3]{3,2,1,0:T(8,128)S(1)} %get-tuple-element.6), channel_id=1, source_target_pairs={{0,1},{2,3},{4,5},{6,7},{8,9},{10,11},{12,13},{14,15},{16,17},{18,... | collective-permute-start | bytes 11528 | tf_op jit(solution)/shard_map/ppermute | solution.py:18
where the time goes:
time: 72.9 us; the launch traced here: 71.7 us
  waiting for transfers between devices  37.4 us (51%)
  starting transfers between devices  17.2 us (24%)
  local copies, waits for them, and re-layouts  8.85 us (12%)
  other arithmetic  4.78 us (7%)
  matrix products  2.53 us (3%)
  between operations  0.89 us (1%)
    all_to_all x1, waiting for transfers between devices, body(): lax.all_to_all(solved, 'ax', split_axis=1, concat_axis=2, tiled=True)  21.1 us
    all_to_all x1, waiting for transfers between devices, body(): lines = lax.all_to_all(flat, 'ax', split_axis=1, concat_axis=0, tiled=True)  15.4 us
    all_to_all x1, starting transfers between devices, body(): lines = lax.all_to_all(flat, 'ax', split_axis=1, concat_axis=0, tiled=True)  8.31 us
    all_to_all x1, starting transfers between devices, body(): lax.all_to_all(solved, 'ax', split_axis=1, concat_axis=2, tiled=True)  4.55 us
    ppermute x1, starting transfers between devices, with_halo(): before = lax.ppermute(last, axis, up)  3.05 us
    all_to_all x2, local copies, waits for them, and re-layouts, body(): lines = lax.all_to_all(flat, 'ax', split_axis=1, concat_axis=0, tiled=True)  2.53 us
    reshape x1, local copies, waits for them, and re-layouts, body(): solved = solved.reshape(2, total, -1)  2.07 us
    div x1, other arithmetic, body(): (45.0 * (radial_cell(1) - radial_cell(-1)) - 9.0 * (radial_cell(2) - radi...  2.02 us
  transfers between devices with their start and end apart: 4, of which 3 were waited for; matrix products, arithmetic and copies ran while one was open for 6% of the time, Pallas kernels for 0%

commit v1 on v0

v1 whole, which is shorter than its diff:
```python
import functools

import jax
import jax.numpy as jnp
import numpy as np
from jax import lax
from jax.experimental import pallas as pl
from jax.experimental.pallas import tpu as pltpu
from jax.sharding import PartitionSpec as P

MESH = pl.DeviceIdType.MESH
ALPHAS = (1.0 / 3.0, 0.4999)
HALO = 3
EDGE = 128


def stage_radices(n):
    radices, m = [], n
    for _ in range(2):
        if m % 2 == 0 and m > 2:
            radices.append(2)
            m //= 2
    while m > 8:
        radix = next(k for k in (4, 2, 3, 5, 7, m) if m % k == 0)
        radices.append(radix)
        m //= radix
    if m > 1:
        radices.append(m)
    return radices


def stencils():
    af = ALPHAS[1]
    a = [
        (93.0 + 70.0 * af) / 128.0,
        (7.0 + 18.0 * af) / 16.0,
        (-7.0 + 14.0 * af) / 32.0,
        (1.0 - 2.0 * af) / 16.0,
        (-1.0 + 2.0 * af) / 128.0,
    ]
    deriv = {1: 7.0 / 9.0, -1: -7.0 / 9.0, 2: 1.0 / 36.0, -2: -1.0 / 36.0}
    filt = {0: a[0]}
    for k in range(1, 5):
        filt[k] = a[k] / 2.0
        filt[-k] = a[k] / 2.0
    return deriv, filt


def operators(n, rows):
    total = n * rows
    result = []
    for alpha, stencil in zip(ALPHAS, stencils()):
        a = np.eye(total) + alpha * (np.eye(total, k=1) + np.eye(total, k=-1))
        b = sum(c * np.eye(total, k=k) for k, c in stencil.items())
        inverse = np.linalg.inv(a)
        dense = inverse @ b
        back, front = np.ones(total), np.ones(total)
        for k in range(1, total):
            front[k] = 1.0 - alpha * alpha / front[k - 1]
            back[total - 1 - k] = 1.0 - alpha * alpha / back[total - k]
        gain_l = np.prod((-alpha / back).reshape(n, rows), axis=1)
        gain_r = np.prod((-alpha / front).reshape(n, rows), axis=1)
        result.append((inverse, dense, gain_l, gain_r))
    return result


class Layout:
    def __init__(self):
        self.size = 0

    def take(self, count):
        at = self.size
        self.size += count
        return at


def coefficients(n, rows, radices):
    ops = operators(n, rows)
    lay = Layout()
    at = {
        "local": lay.take(2 * rows * rows),
        "ul": lay.take(2 * rows),
        "ur": lay.take(2 * rows),
        "er": lay.take(2 * HALO * HALO),
        "el": lay.take(2 * HALO * HALO),
        "sum": lay.take(4 * rows),
        "stage": [lay.take(4 + 8 * (r - 1)) for r in radices],
    }
    table = np.zeros((n, lay.size))
    for d in range(n):
        first, last = d * rows, d * rows + rows - 1
        line = table[d]
        for o, (inverse, dense, gain_l, gain_r) in enumerate(ops):
            own = dense[first : last + 1, first : last + 1]
            line[at["local"] + o * rows * rows :][: rows * rows] = own.reshape(-1)
            ul = inverse[first : last + 1, last]
            ur = inverse[first : last + 1, first]
            line[at["ul"] + o * rows :][:rows] = ul
            line[at["ur"] + o * rows :][:rows] = ur
            if d + 1 < n:
                nxt = slice(last + 1, last + 1 + rows)
                lam = dense[first, nxt] / inverse[first, last]
                table[d + 1, at["sum"] + (2 + o) * rows :][:rows] = lam
                for p in range(HALO):
                    for q in range(p + 1):
                        i = rows - HALO + p
                        value = dense[first + i, last + 1 + q] - ul[i] * lam[q]
                        line[at["er"] + (o * HALO + p) * HALO + q] = value
            if d > 0:
                prev = slice(first - rows, first)
                rho = dense[last, prev] / inverse[last, first]
                table[d - 1, at["sum"] + o * rows :][:rows] = rho
                for p in range(HALO):
                    for q in range(p, HALO):
                        j = rows - HALO + q
                        value = dense[first + p, first - rows + j] - ur[p] * rho[j]
                        line[at["el"] + (o * HALO + p) * HALO + q] = value
            stride = 1
            for s, radix in enumerate(radices):
                where = at["stage"][s]
                digit = (d // stride) % radix
                base = d - d % stride - digit * stride
                end = base + radix * stride
                start = base + digit * stride
                line[where + o] = np.prod(gain_r[start + stride : end])
                line[where + 2 + o] = np.prod(gain_l[base:start])
                for k in range(1, radix):
                    other = (digit - k) % radix
                    begin = base + other * stride
                    stop = begin + stride
                    slot = where + 4 + 8 * (k - 1)
                    if other < digit:
                        line[slot + o] = np.prod(gain_r[stop:d])
                    else:
                        line[slot + 2 + o] = np.prod(gain_l[d + 1 : begin])
                    line[slot + 4 + o] = np.prod(gain_r[stop:end])
                    line[slot + 6 + o] = np.prod(gain_l[base:begin])
                stride *= radix
    return table.astype(np.float32), at


def kernel(n, n_rad, radices, at, table_ref, f_ref, deriv_ref, filt_ref, radial_ref, *scratch):
    stages = len(radices)
    (tab, prefix, halo_l, halo_r, rim_l, rim_r, tab_sem, halo_send, halo_recv, rim_send, rim_recv) = scratch[:11]
    rest = scratch[11:]
    mine, came = rest[:stages], rest[stages : 2 * stages]
    sends, recvs = rest[2 * stages : 3 * stages], rest[3 * stages :]
    rows, fields, planes, width = f_ref.shape
    d = lax.axis_index("ax")
    r = lax.axis_index("rad")

    load = pltpu.make_async_copy(table_ref.at[d], tab, tab_sem)
    load.start()

    def const(index):
        return tab[0, index]

    def partner(s, k):
        stride = 1
        for radix in radices[:s]:
            stride *= radix
        digit = (d // stride) % radices[s]
        other = (digit + k) % radices[s]
        return digit, other, d + (other - digit) * stride

    barrier = pltpu.get_barrier_semaphore()
    fixed = 0
    for s in range(stages):
        for k in range(1, radices[s]):
            pl.semaphore_signal(barrier, inc=1, device_id={"ax": partner(s, k)[2]}, device_id_type=MESH)
            fixed += 1
    near = (
        (d > 0, {"ax": d - 1}),
        (d < n - 1, {"ax": d + 1}),
        (r > 0, {"rad": r - 1}),
        (r < n_rad - 1, {"rad": r + 1}),
    )
    for there, target in near:

        @pl.when(there)
        def _(target=target):
            pl.semaphore_signal(barrier, inc=1, device_id=target, device_id_type=MESH)

    load.wait()

    def sums(c, carry):
        own = [f_ref[j, c] for j in range(rows)]
        for u in range(4):
            acc = const(at["sum"] + u * rows) * own[0]
            for j in range(1, rows):
                acc = acc + const(at["sum"] + u * rows + j) * own[j]
            mine[0][c, u] = acc
        return carry

    lax.fori_loop(0, fields, sums, 0)

    beside = (d + n - 1) // n + (2 * n - 2 - d) // n
    across = (r + n_rad - 1) // n_rad + (2 * n_rad - 2 - r) // n_rad
    pl.semaphore_wait(barrier, fixed + beside + across)

    def stage_copy(s, k, c):
        digit, other, target = partner(s, k)
        if s == stages - 1:
            half = 1 - (other + radices[s] - digit) // radices[s]
            source = mine[s].at[c, pl.ds(2 * half, 2)]
        else:
            source = mine[s].at[c]
        return pltpu.make_async_remote_copy(
            src_ref=source,
            dst_ref=came[s].at[c, k - 1],
            send_sem=sends[s].at[c, k - 1],
            recv_sem=recvs[s].at[c, k - 1],
            device_id={"ax": target},
            device_id_type=MESH,
        )

    def to_right(c):
        return pltpu.make_async_remote_copy(
            src_ref=f_ref.at[pl.ds(rows - HALO, HALO), c],
            dst_ref=halo_l.at[c],
            send_sem=halo_send.at[0, c],
            recv_sem=halo_recv.at[0, c],
            device_id={"ax": d + 1},
            device_id_type=MESH,
        )

    def to_left(c):
        return pltpu.make_async_remote_copy(
            src_ref=f_ref.at[pl.ds(0, HALO), c],
            dst_ref=halo_r.at[c],
            send_sem=halo_send.at[1, c],
            recv_sem=halo_recv.at[1, c],
            device_id={"ax": d - 1},
            device_id_type=MESH,
        )

    rim_right = pltpu.make_async_remote_copy(
        src_ref=f_ref.at[:, :, :, pl.ds(width - EDGE, EDGE)],
        dst_ref=rim_l,
        send_sem=rim_send.at[0],
        recv_sem=rim_recv.at[0],
        device_id={"rad": r + 1},
        device_id_type=MESH,
    )
    rim_left = pltpu.make_async_remote_copy(
        src_ref=f_ref.at[:, :, :, pl.ds(0, EDGE)],
        dst_ref=rim_r,
        send_sem=rim_send.at[1],
        recv_sem=rim_recv.at[1],
        device_id={"rad": r - 1},
        device_id_type=MESH,
    )

    for c in range(fields):
        for k in range(1, radices[0]):
            stage_copy(0, k, c).start()

    @pl.when(r < n_rad - 1)
    def _():
        rim_right.start()

    @pl.when(r > 0)
    def _():
        rim_left.start()

    @pl.when(d < n - 1)
    def _():
        for c in range(fields):
            to_right(c).start()

    @pl.when(d > 0)
    def _():
        for c in range(fields):
            to_left(c).start()

    @pl.when(d == 0)
    def _():
        halo_l[...] = jnp.zeros_like(halo_l)

    @pl.when(d == n - 1)
    def _():
        halo_r[...] = jnp.zeros_like(halo_r)

    @pl.when(r == 0)
    def _():
        rim_l[...] = jnp.zeros_like(rim_l)

    @pl.when(r == n_rad - 1)
    def _():
        rim_r[...] = jnp.zeros_like(rim_r)

    def local(c, carry):
        own = [f_ref[j, c] for j in range(rows)]
        for o, out in enumerate((deriv_ref, filt_ref)):
            for i in range(rows):
                where = at["local"] + (o * rows + i) * rows
                acc = const(where) * own[0]
                for j in range(1, rows):
                    acc = acc + const(where + j) * own[j]
                out[i, c] = acc
        return carry

    lax.fori_loop(0, fields, local, 0)

    @pl.when(r < n_rad - 1)
    def _():
        rim_left.wait_recv()

    @pl.when(r > 0)
    def _():
        rim_right.wait_recv()

    def radial(c):
        def one(i, carry):
            wide = jnp.concatenate([rim_l[i, c], f_ref[i, c], rim_r[i, c]], axis=1)

            def cell(k):
                return wide[:, EDGE + k : EDGE + k + width]

            radial_ref[i, c] = (
                (45.0 / 60.0) * (cell(1) - cell(-1))
                - (9.0 / 60.0) * (cell(2) - cell(-2))
                + (1.0 / 60.0) * (cell(3) - cell(-3))
            )
            return carry

        lax.fori_loop(0, rows, one, 0)

    def step(s, c):
        final = s == stages - 1
        where = at["stage"][s]
        old = None if s == 0 else [prefix[c, u] for u in range(4)]
        grown = None if final else [const(where + u) * mine[s][c, u] for u in range(4)]
        for k in range(1, radices[s]):
            stage_copy(s, k, c).wait_recv()
            slot = where + 4 + 8 * (k - 1)
            got = [came[s][c, k - 1, u] for u in range(2 if final else 4)]
            if final:
                got = got + got
            add = [const(slot + u) * got[u] for u in range(4)]
            old = add if old is None else [a + b for a, b in zip(old, add)]
            if not final:
                grown = [g + const(slot + 4 + u) * got[u] for u, g in enumerate(grown)]
        for u in range(4):
            prefix[c, u] = old[u]
        if not final:
            for u in range(4):
                mine[s + 1][c, u] = grown[u]
            for k in range(1, radices[s + 1]):
                stage_copy(s + 1, k, c).start()

    for t in range(fields + stages - 1):
        for s in range(stages):
            if 0 <= t - s < fields:
                step(s, t - s)
        if t < fields:
            radial(t)

    for c in range(fields):

        @pl.when(d > 0)
        def _(c=c):
            to_right(c).wait_recv()

        @pl.when(d < n - 1)
        def _(c=c):
            to_left(c).wait_recv()

        pre = [prefix[c, u] for u in range(4)]
        left = [halo_l[c, q] for q in range(HALO)]
        right = [halo_r[c, q] for q in range(HALO)]
        for o, out in enumerate((deriv_ref, filt_ref)):
            reach = 1 if o == 0 else HALO
            for i in range(rows):
                acc = out[i, c] + const(at["ur"] + o * rows + i) * pre[o]
                acc = acc + const(at["ul"] + o * rows + i) * pre[2 + o]
                if i < reach:
                    for q in range(HALO - reach + i, HALO):
                        acc = acc + const(at["el"] + (o * HALO + i) * HALO + q) * left[q]
                p = i - (rows - HALO)
                if p >= HALO - reach:
                    for q in range(p - (HALO - reach) + 1):
                        acc = acc + const(at["er"] + (o * HALO + p) * HALO + q) * right[q]
                out[i, c] = acc

    for s in range(stages):
        for c in range(fields):
            for k in range(1, radices[s]):
                stage_copy(s, k, c).wait_send()

    @pl.when(d < n - 1)
    def _():
        for c in range(fields):
            to_right(c).wait_send()

    @pl.when(d > 0)
    def _():
        for c in range(fields):
            to_left(c).wait_send()

    @pl.when(r < n_rad - 1)
    def _():
        rim_right.wait_send()

    @pl.when(r > 0)
    def _():
        rim_left.wait_send()


def solution(mesh):
    n, n_rad = mesh.shape["ax"], mesh.shape["rad"]
    radices = stage_radices(n)

    def body(fields):
        rows, count, planes, width = fields.shape
        table, at = coefficients(n, rows, radices)
        size = table.shape[1]
        unit = (planes, width)
        last = len(radices) - 1
        dma = pltpu.SemaphoreType.DMA
        vmem = functools.partial(pltpu.VMEM, dtype=jnp.float32)
        scratch = [
            pltpu.SMEM((1, size), jnp.float32),
            vmem((count, 4) + unit),
            vmem((count, HALO) + unit),
            vmem((count, HALO) + unit),
            vmem((rows, count, planes, EDGE)),
            vmem((rows, count, planes, EDGE)),
            dma(()),
            dma((2, count)),
            dma((2, count)),
            dma((2,)),
            dma((2,)),
        ]
        scratch += [vmem((count, 4) + unit) for _ in radices]
        scratch += [vmem((count, k - 1, 2 if s == last else 4) + unit) for s, k in enumerate(radices)]
        scratch += [dma((count, k - 1)) for k in radices] * 2
        out = jax.ShapeDtypeStruct(fields.shape, jnp.float32)
        return pl.pallas_call(
            functools.partial(kernel, n, n_rad, radices, at),
            out_shape=(out, out, out),
            in_specs=[pl.BlockSpec(memory_space=pl.ANY), pl.BlockSpec(memory_space=pltpu.VMEM)],
            out_specs=(pl.BlockSpec(memory_space=pltpu.VMEM),) * 3,
            scratch_shapes=scratch,
            compiler_params=pltpu.CompilerParams(
                collective_id=0, has_side_effects=True, vmem_limit_bytes=40 * 1024 * 1024
            ),
        )(jnp.asarray(table).reshape(n, 1, size), fields)

    spec = P("ax", None, None, "rad")
    return jax.shard_map(body, mesh=mesh, in_specs=(spec,), out_specs=(spec,) * 3, check_vma=False)
```

time: 72.9 us -> 43.5 us (0.60); the launches traced: 71.7 us -> 43.3 us
  Pallas kernels: 0 us -> 38.3 us
  waiting for transfers between devices: 37.4 us -> 0 us
  starting transfers between devices: 17.2 us -> 0 us
  other arithmetic: 4.78 us -> 0 us
  local copies, waits for them, and re-layouts: 8.85 us -> 4.33 us
  matrix products: 2.53 us -> 0 us
    pallas_call x0 -> x1, Pallas kernels: none -> 38.3 us  [body(): pl.pallas_call(functools.partial(kernel, n, n_rad, radices, at), out_shap...]
    all_to_all x2 -> x0, waiting for transfers between devices: 36.5 us -> none  [the longest x1 21.1 us: body(): lax.all_to_all(solved, 'ax', split_axis=1, concat_axis=2, tiled=True)]
    all_to_all x2 -> x0, starting transfers between devices: 12.9 us -> none  [the longest x1 8.31 us: body(): lines = lax.all_to_all(flat, 'ax', split_axis=1, concat_axis=0, tiled=True)]
    ppermute x2 -> x0, starting transfers between devices: 4.34 us -> none  [the longest x1 3.05 us: with_halo(): before = lax.ppermute(last, axis, up)]
    unnamed x5 -> x7, local copies, waits for them, and re-layouts: 0.07 us -> 4.33 us
    dot_general x2 -> x0, matrix products: 2.53 us -> none  [the longest x1 1.3 us: solve(): jnp.einsum('sbkj,sbjl->sbkl', backward, eliminated, precision=lax.Precisi...]
    all_to_all x2 -> x0, local copies, waits for them, and re-layouts: 2.53 us -> none  [body(): lines = lax.all_to_all(flat, 'ax', split_axis=1, concat_axis=0, tiled=True)]
    reshape x1 -> x0, local copies, waits for them, and re-layouts: 2.07 us -> none  [body(): solved = solved.reshape(2, total, -1)]
  transfers between devices with their start and end apart: 4 -> 0, of which waited for: 3 -> 0; matrix products, arithmetic and copies ran while one was open for 6% -> 0% of each run, Pallas kernels for 0% -> 0%
where the time goes in v1:
time: 43.5 us; the launch traced here: 43.3 us
  Pallas kernels  38.3 us (88%)
  local copies, waits for them, and re-layouts  4.33 us (10%)
  between operations  0.65 us (1%)
    pallas_call x1, Pallas kernels, body(): pl.pallas_call(functools.partial(kernel, n, n_rad, radices, at), out_shap...  38.3 us
    unnamed x7, local copies, waits for them, and re-layouts  4.33 us

profile of v1, /device:TPU:0, one launch (start us, length us, event | category | flops | bytes accessed | tf_op | source)
XLA Modules:
  0.0 43.3 jit_solution(8804116273960777049)
XLA Ops:
  0.6 0.0 copy-start
  0.6 1.1 %copy-done = f32[8,5,8,512]{3,2,1,0:T(8,128)S(1)} copy-done((f32[8,5,8,512]{3,2,1,0:T(8,128)S(1)}, f32[8,5,8,512]{3,2,1,0:T(8,128)}, u32[]{:S(2)}) %copy-start) | copy-done | bytes 655384
  1.7 0.0 copy-start.1
  1.7 0.7 %copy-done.1 = f32[16,1,280]{2,1,0:T(1,128)S(1)} copy-done((f32[16,1,280]{2,1,0:T(1,128)S(1)}, f32[16,1,280]{2,1,0:T(1,128)}, u32[]{:S(2)}) %copy-start.1) | copy-done | bytes 17944
  2.5 38.3 %shard_map.49 = (f32[8,5,8,512]{3,2,1,0:T(8,128)S(1)}, f32[8,5,8,512]{3,2,1,0:T(8,128)S(1)}, f32[8,5,8,512]{3,2,1,0:T(8,128)S(1)}) custom-call(f32[16,1,280]{2,1,0:T(1,128)S(1)} %copy-done.1, f32[8,5,8,512]{3,2,1,0:T(8,128)S(1)} %copy-done), custom_call_target="tpu_custom_call" | custom-call | tf_op jit(solution)/shard_map/pallas_call | solution.py:439
  40.8 0.8 %copy.8 = f32[8,5,8,512]{3,2,1,0:T(8,128)} copy(f32[8,5,8,512]{3,2,1,0:T(8,128)S(1)} %get-tuple-element.6) | data formatting | bytes 1310720
  41.6 0.8 %copy.9 = f32[8,5,8,512]{3,2,1,0:T(8,128)} copy(f32[8,5,8,512]{3,2,1,0:T(8,128)S(1)} %get-tuple-element.7) | data formatting | bytes 1310720
  42.4 0.8 %copy.10 = f32[8,5,8,512]{3,2,1,0:T(8,128)} copy(f32[8,5,8,512]{3,2,1,0:T(8,128)S(1)} %get-tuple-element.8) | data formatting | bytes 1310720
Async XLA Ops:
  0.6 1.1 %copy-start = (f32[8,5,8,512]{3,2,1,0:T(8,128)S(1)}, f32[8,5,8,512]{3,2,1,0:T(8,128)}, u32[]{:S(2)}) copy-start(f32[8,5,8,512]{3,2,1,0:T(8,128)} %f_ref.1) | copy-start | bytes 1966084
  1.7 0.7 %copy-start.1 = (f32[16,1,280]{2,1,0:T(1,128)S(1)}, f32[16,1,280]{2,1,0:T(1,128)}, u32[]{:S(2)}) copy-start(f32[16,1,280]{2,1,0:T(1,128)} %constant.4.table_ref) | copy-start | bytes 53764

commit v2 on v1

--- a/solution.py
+++ b/solution.py
@@ -16,16 +16,10 @@
 
 def stage_radices(n):
     radices, m = [], n
-    for _ in range(2):
-        if m % 2 == 0 and m > 2:
-            radices.append(2)
-            m //= 2
-    while m > 8:
-        radix = next(k for k in (4, 2, 3, 5, 7, m) if m % k == 0)
+    while m > 1:
+        radix = next(k for k in range(2, m + 1) if m % k == 0)
         radices.append(radix)
         m //= radix
-    if m > 1:
-        radices.append(m)
     return radices
 
 
@@ -139,10 +133,11 @@
     return table.astype(np.float32), at
 
 
-def kernel(n, n_rad, radices, at, table_ref, f_ref, deriv_ref, filt_ref, radial_ref, *scratch):
+def kernel(n, n_rad, radices, at, table_ref, fields_ref, deriv_ref, filt_ref, radial_ref, *scratch):
     stages = len(radices)
-    (tab, prefix, halo_l, halo_r, rim_l, rim_r, tab_sem, halo_send, halo_recv, rim_send, rim_recv) = scratch[:11]
-    rest = scratch[11:]
+    (f_ref, tab, prefix, halo_l, halo_r, rim_l, rim_r) = scratch[:7]
+    (f_sem, tab_sem, halo_send, halo_recv, rim_send, rim_recv) = scratch[7:13]
+    rest = scratch[13:]
     mine, came = rest[:stages], rest[stages : 2 * stages]
     sends, recvs = rest[2 * stages : 3 * stages], rest[3 * stages :]
     rows, fields, planes, width = f_ref.shape
@@ -151,6 +146,12 @@
 
     load = pltpu.make_async_copy(table_ref.at[d], tab, tab_sem)
     load.start()
+
+    def fetch(c):
+        return pltpu.make_async_copy(fields_ref.at[:, c], f_ref.at[:, c], f_sem.at[c])
+
+    for c in range(fields):
+        fetch(c).start()
 
     def const(index):
         return tab[0, index]
@@ -181,9 +182,26 @@
         def _(target=target):
             pl.semaphore_signal(barrier, inc=1, device_id=target, device_id_type=MESH)
 
+    @pl.when(d == 0)
+    def _():
+        halo_l[...] = jnp.zeros_like(halo_l)
+
+    @pl.when(d == n - 1)
+    def _():
+        halo_r[...] = jnp.zeros_like(halo_r)
+
+    @pl.when(r == 0)
+    def _():
+        rim_l[...] = jnp.zeros_like(rim_l)
+
+    @pl.when(r == n_rad - 1)
+    def _():
+        rim_r[...] = jnp.zeros_like(rim_r)
+
     load.wait()
 
     def sums(c, carry):
+        fetch(c).wait()
         own = [f_ref[j, c] for j in range(rows)]
         for u in range(4):
             acc = const(at["sum"] + u * rows) * own[0]
@@ -251,43 +269,17 @@
         device_id_type=MESH,
     )
 
+    @pl.when(r < n_rad - 1)
+    def _():
+        rim_right.start()
+
+    @pl.when(r > 0)
+    def _():
+        rim_left.start()
+
     for c in range(fields):
         for k in range(1, radices[0]):
             stage_copy(0, k, c).start()
-
-    @pl.when(r < n_rad - 1)
-    def _():
-        rim_right.start()
-
-    @pl.when(r > 0)
-    def _():
-        rim_left.start()
-
-    @pl.when(d < n - 1)
-    def _():
-        for c in range(fields):
-            to_right(c).start()
-
-    @pl.when(d > 0)
-    def _():
-        for c in range(fields):
-            to_left(c).start()
-
-    @pl.when(d == 0)
-    def _():
-        halo_l[...] = jnp.zeros_like(halo_l)
-
-    @pl.when(d == n - 1)
-    def _():
-        halo_r[...] = jnp.zeros_like(halo_r)
-
-    @pl.when(r == 0)
-    def _():
-        rim_l[...] = jnp.zeros_like(rim_l)
-
-    @pl.when(r == n_rad - 1)
-    def _():
-        rim_r[...] = jnp.zeros_like(rim_r)
 
     def local(c, carry):
         own = [f_ref[j, c] for j in range(rows)]
@@ -301,14 +293,6 @@
         return carry
 
     lax.fori_loop(0, fields, local, 0)
-
-    @pl.when(r < n_rad - 1)
-    def _():
-        rim_left.wait_recv()
-
-    @pl.when(r > 0)
-    def _():
-        rim_right.wait_recv()
 
     def radial(c):
         def one(i, carry):
@@ -349,10 +333,31 @@
             for k in range(1, radices[s + 1]):
                 stage_copy(s + 1, k, c).start()
 
+    def halos(c):
+        @pl.when(d < n - 1)
+        def _():
+            to_right(c).start()
+
+        @pl.when(d > 0)
+        def _():
+            to_left(c).start()
+
     for t in range(fields + stages - 1):
         for s in range(stages):
             if 0 <= t - s < fields:
                 step(s, t - s)
+        if t < fields:
+            halos(t)
+        if t == 0:
+
+            @pl.when(r < n_rad - 1)
+            def _():
+                rim_left.wait_recv()
+
+            @pl.when(r > 0)
+            def _():
+                rim_right.wait_recv()
+
         if t < fields:
             radial(t)
 
@@ -407,6 +412,17 @@
         rim_left.wait_send()
 
 
+def store(a, b, c, out_a, out_b, out_c, sem):
+    copies = [
+        pltpu.make_async_copy(src, dst, sem.at[i])
+        for i, (src, dst) in enumerate(((a, out_a), (b, out_b), (c, out_c)))
+    ]
+    for copy in copies:
+        copy.start()
+    for copy in copies:
+        copy.wait()
+
+
 def solution(mesh):
     n, n_rad = mesh.shape["ax"], mesh.shape["rad"]
     radices = stage_radices(n)
@@ -420,12 +436,14 @@
         dma = pltpu.SemaphoreType.DMA
         vmem = functools.partial(pltpu.VMEM, dtype=jnp.float32)
         scratch = [
+            vmem(fields.shape),
             pltpu.SMEM((1, size), jnp.float32),
             vmem((count, 4) + unit),
             vmem((count, HALO) + unit),
             vmem((count, HALO) + unit),
             vmem((rows, count, planes, EDGE)),
             vmem((rows, count, planes, EDGE)),
+            dma((count,)),
             dma(()),
             dma((2, count)),
             dma((2, count)),
@@ -436,16 +454,24 @@
         scratch += [vmem((count, k - 1, 2 if s == last else 4) + unit) for s, k in enumerate(radices)]
         scratch += [dma((count, k - 1)) for k in radices] * 2
         out = jax.ShapeDtypeStruct(fields.shape, jnp.float32)
-        return pl.pallas_call(
+        solved = pl.pallas_call(
             functools.partial(kernel, n, n_rad, radices, at),
             out_shape=(out, out, out),
-            in_specs=[pl.BlockSpec(memory_space=pl.ANY), pl.BlockSpec(memory_space=pltpu.VMEM)],
+            in_specs=[pl.BlockSpec(memory_space=pltpu.HBM)] * 2,
             out_specs=(pl.BlockSpec(memory_space=pltpu.VMEM),) * 3,
             scratch_shapes=scratch,
             compiler_params=pltpu.CompilerParams(
                 collective_id=0, has_side_effects=True, vmem_limit_bytes=40 * 1024 * 1024
             ),
         )(jnp.asarray(table).reshape(n, 1, size), fields)
+        return pl.pallas_call(
+            store,
+            out_shape=(out, out, out),
+            in_specs=[pl.BlockSpec(memory_space=pltpu.VMEM)] * 3,
+            out_specs=(pl.BlockSpec(memory_space=pltpu.HBM),) * 3,
+            scratch_shapes=[dma((3,))],
+            compiler_params=pltpu.CompilerParams(vmem_limit_bytes=4 * 1024 * 1024),
+        )(*solved)
 
     spec = P("ax", None, None, "rad")
     return jax.shard_map(body, mesh=mesh, in_specs=(spec,), out_specs=(spec,) * 3, check_vma=False)

time: 43.5 us -> 37.2 us (0.86); the launches traced: 43.3 us -> 36.5 us
  Pallas kernels: 38.3 us -> 34.1 us
  local copies, waits for them, and re-layouts: 4.33 us -> 1.82 us
    pallas_call x1, Pallas kernels: 38.3 us -> 32.8 us  [body(): pl.pallas_call(functools.partial(kernel, n, n_rad, radices, at), out_shap...]
    unnamed x7 -> x4, local copies, waits for them, and re-layouts: 4.33 us -> 1.82 us
    pallas_call x0 -> x1, Pallas kernels: none -> 1.3 us  [body(): pl.pallas_call(store, out_shape=(out, out, out), in_specs=[pl.BlockSpec(m...]
where the time goes in v2:
time: 37.2 us; the launch traced here: 36.5 us
  Pallas kernels  34.1 us (92%)
  local copies, waits for them, and re-layouts  1.82 us (5%)
  between operations  0.65 us (2%)
    pallas_call x1, Pallas kernels, body(): pl.pallas_call(functools.partial(kernel, n, n_rad, radices, at), out_shap...  32.8 us
    unnamed x4, local copies, waits for them, and re-layouts  1.82 us
    pallas_call x1, Pallas kernels, body(): pl.pallas_call(store, out_shape=(out, out, out), in_specs=[pl.BlockSpec(m...  1.3 us

profile of v2, /device:TPU:0, one launch (start us, length us, event | category | flops | bytes accessed | tf_op | source)
XLA Modules:
  0.0 36.5 jit_solution(18009579915049965503)
XLA Ops:
  0.6 0.0 copy-start
  0.6 1.1 %copy-done = f32[8,5,8,512]{3,2,1,0:T(8,128)S(1)} copy-done((f32[8,5,8,512]{3,2,1,0:T(8,128)S(1)}, f32[8,5,8,512]{3,2,1,0:T(8,128)}, u32[]{:S(2)}) %copy-start) | copy-done | bytes 655384
  1.7 0.0 copy-start.1
  1.7 0.7 %copy-done.1 = f32[16,1,276]{2,1,0:T(1,128)S(1)} copy-done((f32[16,1,276]{2,1,0:T(1,128)S(1)}, f32[16,1,276]{2,1,0:T(1,128)}, u32[]{:S(2)}) %copy-start.1) | copy-done | bytes 17688
  2.5 32.8 %shard_map.49 = (f32[8,5,8,512]{3,2,1,0:T(8,128)S(1)}, f32[8,5,8,512]{3,2,1,0:T(8,128)S(1)}, f32[8,5,8,512]{3,2,1,0:T(8,128)S(1)}) custom-call(f32[16,1,276]{2,1,0:T(1,128)S(1)} %copy-done.1, f32[8,5,8,512]{3,2,1,0:T(8,128)S(1)} %copy-done), custom_call_target="tpu_custom_call" | custom-call | tf_op jit(solution)/shard_map/pallas_call | solution.py:457
  35.3 1.3 %shard_map.50 = (f32[8,5,8,512]{3,2,1,0:T(8,128)}, f32[8,5,8,512]{3,2,1,0:T(8,128)}, f32[8,5,8,512]{3,2,1,0:T(8,128)}) custom-call(f32[8,5,8,512]{3,2,1,0:T(8,128)S(1)} %get-tuple-element.6.a, f32[8,5,8,512]{3,2,1,0:T(8,128)S(1)} %get-tuple-element.7.b, f32[8,5,8,512]{3,2,1,0:T(8,128)S(1)} %get-tuple-element.8.c), custom_call_target="tpu_custom_call" | custom-call | tf_op jit(solution)/shard_map/pallas_call | solution.py:467
Async XLA Ops:
  0.6 1.1 %copy-start = (f32[8,5,8,512]{3,2,1,0:T(8,128)S(1)}, f32[8,5,8,512]{3,2,1,0:T(8,128)}, u32[]{:S(2)}) copy-start(f32[8,5,8,512]{3,2,1,0:T(8,128)} %fields_ref.1) | copy-start | bytes 1966084
  1.7 0.7 %copy-start.1 = (f32[16,1,276]{2,1,0:T(1,128)S(1)}, f32[16,1,276]{2,1,0:T(1,128)}, u32[]{:S(2)}) copy-start(f32[16,1,276]{2,1,0:T(1,128)} %constant.4.table_ref) | copy-start | bytes 52996

commit v3 on v2

--- a/solution.py
+++ b/solution.py
@@ -12,6 +12,11 @@
 ALPHAS = (1.0 / 3.0, 0.4999)
 HALO = 3
 EDGE = 128
+SPLIT = 1
+SKEW = 2.0
+HALO_AT = 0.1
+LOCAL_AT = -5.0
+RADIAL_AT = 1.2
 
 
 def stage_radices(n):
@@ -133,25 +138,22 @@
     return table.astype(np.float32), at
 
 
-def kernel(n, n_rad, radices, at, table_ref, fields_ref, deriv_ref, filt_ref, radial_ref, *scratch):
+def kernel(n, n_rad, radices, at, table_ref, f_ref, deriv_ref, filt_ref, radial_ref, *scratch):
     stages = len(radices)
-    (f_ref, tab, prefix, halo_l, halo_r, rim_l, rim_r) = scratch[:7]
-    (f_sem, tab_sem, halo_send, halo_recv, rim_send, rim_recv) = scratch[7:13]
-    rest = scratch[13:]
+    (tab, prefix, halo_l, halo_r, rim_l, rim_r) = scratch[:6]
+    (tab_sem, halo_send, halo_recv, rim_send, rim_recv) = scratch[6:11]
+    rest = scratch[11:]
     mine, came = rest[:stages], rest[stages : 2 * stages]
     sends, recvs = rest[2 * stages : 3 * stages], rest[3 * stages :]
     rows, fields, planes, width = f_ref.shape
+    pieces = fields * SPLIT
+    part = width // SPLIT
+    lanes = [slice(h * part, (h + 1) * part) for h in range(SPLIT)]
     d = lax.axis_index("ax")
     r = lax.axis_index("rad")
 
     load = pltpu.make_async_copy(table_ref.at[d], tab, tab_sem)
     load.start()
-
-    def fetch(c):
-        return pltpu.make_async_copy(fields_ref.at[:, c], f_ref.at[:, c], f_sem.at[c])
-
-    for c in range(fields):
-        fetch(c).start()
 
     def const(index):
         return tab[0, index]
@@ -201,13 +203,13 @@
     load.wait()
 
     def sums(c, carry):
-        fetch(c).wait()
         own = [f_ref[j, c] for j in range(rows)]
         for u in range(4):
             acc = const(at["sum"] + u * rows) * own[0]
             for j in range(1, rows):
                 acc = acc + const(at["sum"] + u * rows + j) * own[j]
-            mine[0][c, u] = acc
+            for h in range(SPLIT):
+                mine[0][c * SPLIT + h, u] = acc[:, lanes[h]]
         return carry
 
     lax.fori_loop(0, fields, sums, 0)
@@ -277,7 +279,7 @@
     def _():
         rim_left.start()
 
-    for c in range(fields):
+    for c in range(pieces):
         for k in range(1, radices[0]):
             stage_copy(0, k, c).start()
 
@@ -292,7 +294,8 @@
                 out[i, c] = acc
         return carry
 
-    lax.fori_loop(0, fields, local, 0)
+    def local_part(c):
+        lax.fori_loop(c, c + 1, local, 0)
 
     def radial(c):
         def one(i, carry):
@@ -342,24 +345,22 @@
         def _():
             to_left(c).start()
 
-    for t in range(fields + stages - 1):
-        for s in range(stages):
-            if 0 <= t - s < fields:
-                step(s, t - s)
-        if t < fields:
-            halos(t)
-        if t == 0:
-
-            @pl.when(r < n_rad - 1)
-            def _():
-                rim_left.wait_recv()
-
-            @pl.when(r > 0)
-            def _():
-                rim_right.wait_recv()
-
-        if t < fields:
-            radial(t)
+    def rim_wait():
+        @pl.when(r < n_rad - 1)
+        def _():
+            rim_left.wait_recv()
+
+        @pl.when(r > 0)
+        def _():
+            rim_right.wait_recv()
+
+    events = [(c / SPLIT + SKEW * s, functools.partial(step, s, c)) for s in range(stages) for c in range(pieces)]
+    events += [(c + HALO_AT, functools.partial(halos, c)) for c in range(fields)]
+    events += [(c + LOCAL_AT, functools.partial(local_part, c)) for c in range(fields)]
+    events += [(c + RADIAL_AT, functools.partial(radial, c)) for c in range(fields)]
+    events.append((RADIAL_AT - 0.01, rim_wait))
+    for _, event in sorted(events, key=lambda item: item[0]):
+        event()
 
     for c in range(fields):
 
@@ -371,25 +372,26 @@
         def _(c=c):
             to_left(c).wait_recv()
 
-        pre = [prefix[c, u] for u in range(4)]
-        left = [halo_l[c, q] for q in range(HALO)]
-        right = [halo_r[c, q] for q in range(HALO)]
-        for o, out in enumerate((deriv_ref, filt_ref)):
-            reach = 1 if o == 0 else HALO
-            for i in range(rows):
-                acc = out[i, c] + const(at["ur"] + o * rows + i) * pre[o]
-                acc = acc + const(at["ul"] + o * rows + i) * pre[2 + o]
-                if i < reach:
-                    for q in range(HALO - reach + i, HALO):
-                        acc = acc + const(at["el"] + (o * HALO + i) * HALO + q) * left[q]
-                p = i - (rows - HALO)
-                if p >= HALO - reach:
-                    for q in range(p - (HALO - reach) + 1):
-                        acc = acc + const(at["er"] + (o * HALO + p) * HALO + q) * right[q]
-                out[i, c] = acc
+        for h, cut in enumerate(lanes):
+            pre = [prefix[c * SPLIT + h, u] for u in range(4)]
+            left = [halo_l[c, q, :, cut] for q in range(HALO)]
+            right = [halo_r[c, q, :, cut] for q in range(HALO)]
+            for o, out in enumerate((deriv_ref, filt_ref)):
+                reach = 1 if o == 0 else HALO
+                for i in range(rows):
+                    acc = out[i, c, :, cut] + const(at["ur"] + o * rows + i) * pre[o]
+                    acc = acc + const(at["ul"] + o * rows + i) * pre[2 + o]
+                    if i < reach:
+                        for q in range(HALO - reach + i, HALO):
+                            acc = acc + const(at["el"] + (o * HALO + i) * HALO + q) * left[q]
+                    p = i - (rows - HALO)
+                    if p >= HALO - reach:
+                        for q in range(p - (HALO - reach) + 1):
+                            acc = acc + const(at["er"] + (o * HALO + p) * HALO + q) * right[q]
+                    out[i, c, :, cut] = acc
 
     for s in range(stages):
-        for c in range(fields):
+        for c in range(pieces):
             for k in range(1, radices[s]):
                 stage_copy(s, k, c).wait_send()
 
@@ -431,33 +433,31 @@
         rows, count, planes, width = fields.shape
         table, at = coefficients(n, rows, radices)
         size = table.shape[1]
-        unit = (planes, width)
+        whole, unit, pieces = (planes, width), (planes, width // SPLIT), count * SPLIT
         last = len(radices) - 1
         dma = pltpu.SemaphoreType.DMA
         vmem = functools.partial(pltpu.VMEM, dtype=jnp.float32)
         scratch = [
-            vmem(fields.shape),
             pltpu.SMEM((1, size), jnp.float32),
-            vmem((count, 4) + unit),
-            vmem((count, HALO) + unit),
-            vmem((count, HALO) + unit),
+            vmem((pieces, 4) + unit),
+            vmem((count, HALO) + whole),
+            vmem((count, HALO) + whole),
             vmem((rows, count, planes, EDGE)),
             vmem((rows, count, planes, EDGE)),
-            dma((count,)),
             dma(()),
             dma((2, count)),
             dma((2, count)),
             dma((2,)),
             dma((2,)),
         ]
-        scratch += [vmem((count, 4) + unit) for _ in radices]
-        scratch += [vmem((count, k - 1, 2 if s == last else 4) + unit) for s, k in enumerate(radices)]
-        scratch += [dma((count, k - 1)) for k in radices] * 2
+        scratch += [vmem((pieces, 4) + unit) for _ in radices]
+        scratch += [vmem((pieces, k - 1, 2 if s == last else 4) + unit) for s, k in enumerate(radices)]
+        scratch += [dma((pieces, k - 1)) for k in radices] * 2
         out = jax.ShapeDtypeStruct(fields.shape, jnp.float32)
         solved = pl.pallas_call(
             functools.partial(kernel, n, n_rad, radices, at),
             out_shape=(out, out, out),
-            in_specs=[pl.BlockSpec(memory_space=pltpu.HBM)] * 2,
+            in_specs=[pl.BlockSpec(memory_space=pltpu.HBM), pl.BlockSpec(memory_space=pltpu.VMEM)],
             out_specs=(pl.BlockSpec(memory_space=pltpu.VMEM),) * 3,
             scratch_shapes=scratch,
             compiler_params=pltpu.CompilerParams(

time: 37.2 us -> 34.5 us (0.927); the launches traced: 36.5 us -> 34.3 us
  Pallas kernels: 34.1 us -> 31.8 us
    pallas_call x1, Pallas kernels: 32.8 us -> 30.5 us  [body(): pl.pallas_call(functools.partial(kernel, n, n_rad, radices, at), out_shap...]
where the time goes in v3:
time: 34.5 us; the launch traced here: 34.3 us
  Pallas kernels  31.8 us (92%)
  local copies, waits for them, and re-layouts  1.82 us (5%)
  between operations  0.65 us (2%)
    pallas_call x1, Pallas kernels, body(): pl.pallas_call(functools.partial(kernel, n, n_rad, radices, at), out_shap...  30.5 us
    unnamed x4, local copies, waits for them, and re-layouts  1.82 us
    pallas_call x1, Pallas kernels, body(): pl.pallas_call(store, out_shape=(out, out, out), in_specs=[pl.BlockSpec(m...  1.3 us

profile of v3, /device:TPU:0, one launch (start us, length us, event | category | flops | bytes accessed | tf_op | source)
XLA Modules:
  0.0 34.3 jit_solution(7443929685398383889)
XLA Ops:
  0.6 0.0 copy-start
  0.6 1.1 %copy-done = f32[8,5,8,512]{3,2,1,0:T(8,128)S(1)} copy-done((f32[8,5,8,512]{3,2,1,0:T(8,128)S(1)}, f32[8,5,8,512]{3,2,1,0:T(8,128)}, u32[]{:S(2)}) %copy-start) | copy-done | bytes 655384
  1.7 0.0 copy-start.1
  1.7 0.7 %copy-done.1 = f32[16,1,276]{2,1,0:T(1,128)S(1)} copy-done((f32[16,1,276]{2,1,0:T(1,128)S(1)}, f32[16,1,276]{2,1,0:T(1,128)}, u32[]{:S(2)}) %copy-start.1) | copy-done | bytes 17688
  2.5 30.5 %shard_map.49 = (f32[8,5,8,512]{3,2,1,0:T(8,128)S(1)}, f32[8,5,8,512]{3,2,1,0:T(8,128)S(1)}, f32[8,5,8,512]{3,2,1,0:T(8,128)S(1)}) custom-call(f32[16,1,276]{2,1,0:T(1,128)S(1)} %copy-done.1, f32[8,5,8,512]{3,2,1,0:T(8,128)S(1)} %copy-done), custom_call_target="tpu_custom_call" | custom-call | tf_op jit(solution)/shard_map/pallas_call | solution.py:457
  33.0 1.3 %shard_map.50 = (f32[8,5,8,512]{3,2,1,0:T(8,128)}, f32[8,5,8,512]{3,2,1,0:T(8,128)}, f32[8,5,8,512]{3,2,1,0:T(8,128)}) custom-call(f32[8,5,8,512]{3,2,1,0:T(8,128)S(1)} %get-tuple-element.6.a, f32[8,5,8,512]{3,2,1,0:T(8,128)S(1)} %get-tuple-element.7.b, f32[8,5,8,512]{3,2,1,0:T(8,128)S(1)} %get-tuple-element.8.c), custom_call_target="tpu_custom_call" | custom-call | tf_op jit(solution)/shard_map/pallas_call | solution.py:467
Async XLA Ops:
  0.6 1.1 %copy-start = (f32[8,5,8,512]{3,2,1,0:T(8,128)S(1)}, f32[8,5,8,512]{3,2,1,0:T(8,128)}, u32[]{:S(2)}) copy-start(f32[8,5,8,512]{3,2,1,0:T(8,128)} %f_ref.1) | copy-start | bytes 1966084
  1.7 0.7 %copy-start.1 = (f32[16,1,276]{2,1,0:T(1,128)S(1)}, f32[16,1,276]{2,1,0:T(1,128)}, u32[]{:S(2)}) copy-start(f32[16,1,276]{2,1,0:T(1,128)} %constant.4.table_ref) | copy-start | bytes 52996
